TPU v7x, 128 devices: a whole 4x4x4 slice. The times are simulated.
128 devices in a mesh: gx: 8 (over y_hi, z), gy: 4 (over y_lo, core), gz: 4 (over x).
Axes of the slice: x: 4, y: 4 (y_hi: 2, y_lo: 2; y = y_hi * 2 + y_lo), z: 4, core: 2. Of those that a mesh axis runs over, the one named last changes fastest.
Arguments:
- popul: float32 [8, 4, 4, 456, 1152], P('gx', 'gy', 'gz'), may hold values from 0.2 to 0.8
- codes: int32 [256], P(('gx', 'gy', 'gz')), may hold values from 1 to 4, as said below
- solid: int32 [8, 4, 4, 24, 1152], P('gx', 'gy', 'gz'), may hold values 0 or 1
Outputs:
- fields: float32 [8, 4, 4, 456, 1152], P('gx', 'gy', 'gz')
Inputs may be any that keep to these rules, and one draw needn't show every extreme that they name: code // 2 - 1 is the change of device number (in the order gx, gy, gz, cyclic) that the block takes and code % 2 its place there; the codes put every block at exactly one home place; blocks moving to the next device take place 0 there, those moving to the previous one take place 1 there; between some two consecutive devices exactly 1 block move each way.
All inputs are finite; a program needn't handle non-finite values. No bound on the sum of `solid` on one device may be relied on, other than what follows from the above.
Results may differ from a plain program's by a relative error of at most 0.0001.
Values sent between devices are 32-bit elements; how exact they have to be, the bound alone decides.
A program may use at most 128 MiB of HBM per device.

v0:
```python
import jax
import jax.numpy as jnp
from jax import lax
from jax.sharding import PartitionSpec as P

STEPS = 2


VELS = [
    (0, 0, 0),
    (1, 0, 0),
    (-1, 0, 0),
    (0, 1, 0),
    (0, -1, 0),
    (0, 0, 1),
    (0, 0, -1),
    (1, 1, 0),
    (-1, -1, 0),
    (1, -1, 0),
    (-1, 1, 0),
    (1, 0, 1),
    (-1, 0, -1),
    (1, 0, -1),
    (-1, 0, 1),
    (0, 1, 1),
    (0, -1, -1),
    (0, 1, -1),
    (0, -1, 1),
]
WEIGHTS = [1.0 / 3.0] + [1.0 / 18.0] * 6 + [1.0 / 36.0] * 12
OPPOSITE = [VELS.index((-a, -b, -c)) for a, b, c in VELS]
OMEGA = 1.25


def from_behind(shard, axis, by):
    devices = lax.axis_size(axis)
    return lax.ppermute(shard, axis, [(i, (i + by) % devices) for i in range(devices)])


def extended(shard, sides, width):
    for axis, dim in sides:
        devices, length = (lax.axis_size(axis), shard.shape[dim])
        up = [(i, (i + 1) % devices) for i in range(devices)]
        down = [(j, i) for i, j in up]
        last = lax.slice_in_dim(shard, length - width, length, axis=dim)
        initial = lax.slice_in_dim(shard, 0, width, axis=dim)
        before = lax.ppermute(last, axis, up)
        after = lax.ppermute(initial, axis, down)
        shard = jnp.concatenate([before, shard, after], axis=dim)
    return shard


def collide(f, solid_cells):
    rho = sum((f[i] for i in range(19)))
    mom_x = sum((VELS[i][0] * f[i] for i in range(19) if VELS[i][0] != 0))
    mom_y = sum((VELS[i][1] * f[i] for i in range(19) if VELS[i][1] != 0))
    mom_z = sum((VELS[i][2] * f[i] for i in range(19) if VELS[i][2] != 0))
    vel_x = mom_x / rho
    vel_y = mom_y / rho
    vel_z = mom_z / rho
    speed = vel_x * vel_x + vel_y * vel_y + vel_z * vel_z
    posts = []
    for i in range(19):
        along = VELS[i][0] * vel_x + VELS[i][1] * vel_y + VELS[i][2] * vel_z
        equil = WEIGHTS[i] * rho * (1.0 + 3.0 * along + 4.5 * along * along - 1.5 * speed)
        posts.append(f[i] - OMEGA * (f[i] - equil))
    fluid = jnp.stack(posts)
    bounced = jnp.stack([f[o] for o in OPPOSITE])
    return jnp.where(solid_cells[None] == 1, bounced, fluid)


def stream(padded):
    size_x = padded.shape[1] - 2
    size_y = padded.shape[2] - 2
    size_z = padded.shape[3] - 2
    moved = []
    for i in range(19):
        off_x = 1 - VELS[i][0]
        off_y = 1 - VELS[i][1]
        off_z = 1 - VELS[i][2]
        moved.append(
            padded[i, off_x : off_x + size_x, off_y : off_y + size_y, off_z : off_z + size_z]
        )
    return jnp.stack(moved)


def select(table, blocks):
    return jnp.einsum("ks,cxysz->cxykz", table, blocks, precision=lax.Precision.HIGHEST)


def per_device(popul, codes, solid):
    edge = solid.shape[3]
    count = codes.shape[0]
    cells = popul.reshape(19, edge, edge, count * edge)
    solid_cells = solid.reshape(edge, edge, count * edge)
    blocks = cells.reshape(19, edge, edge, count, edge)
    places = jnp.arange(count, dtype=jnp.int32)
    own_table = (codes[None, :] == count + places[:, None]).astype(jnp.float32)
    home = select(own_table, blocks)
    lower_pop, lower_codes = from_behind((cells, codes), ("gx", "gy", "gz"), 1)
    upper_pop, upper_codes = from_behind((cells, codes), ("gx", "gy", "gz"), -1)
    lower_table = (lower_codes[None, :] == 2 * count + places[:, None]).astype(jnp.float32)
    upper_table = (upper_codes[None, :] == places[:, None]).astype(jnp.float32)
    home = home + select(lower_table, lower_pop.reshape(19, edge, edge, count, edge))
    home = home + select(upper_table, upper_pop.reshape(19, edge, edge, count, edge))
    fields = home.reshape(19, edge, edge, count * edge)
    for step in range(STEPS):
        post = collide(fields, solid_cells)
        padded = extended(post, (("gx", 1), ("gy", 2), ("gz", 3)), 1)
        fields = stream(padded)
    return fields.reshape(1, 1, 1, 19 * edge, edge * count * edge)


def solution(mesh):
    placed = (
        P("gx", "gy", "gz", None, None),
        P(("gx", "gy", "gz")),
        P("gx", "gy", "gz", None, None),
    )
    return jax.shard_map(
        per_device,
        mesh=mesh,
        in_specs=placed,
        out_specs=P("gx", "gy", "gz", None, None),
        check_vma=False,
    )
```

profile of v0, /device:TPU:1, one launch (start us, length us, event | category | flops | bytes accessed | tf_op | source)
XLA Modules:
  0.0 420.3 jit_solution(8525806464176026766)
XLA Ops:
  0.0 5.5 %reshape.4301 = f32[19,24,24,48]{3,2,1,0:T(8,128)} reshape(f32[1,1,1,456,1152]{4,3,2,1,0:T(8,128)} %param.3) | data formatting | bytes 4202496 | tf_op jit(solution)/shard_map/reshape | solution.py:94
  9.4 3.3 collective-permute-start.2
  12.7 19.8 %reshape_reshape.3 = f32[19,24,24,2,24]{4,3,2,1,0:T(2,128)} reshape(f32[1,1,1,456,1152]{4,3,2,1,0:T(8,128)S(1)} %copy-done.3) | data formatting | bytes 4202496 | tf_op jit(solution)/shard_map/reshape;reshape | solution.py:96
  33.4 25.3 %fusion.275 = f32[2,19,24,24,24]{4,0,3,2,1:T(2,128)} fusion(f32[19,24,24,2,24]{4,3,2,1,0:T(2,128)} %reshape_reshape.3, s32[2]{0:T(128)S(1)} %copy-done.12, s32[2]{0:T(128)S(1)} %iota_add_fusion.1), kind=kOutput, calls=%fused_computation.446 | convolution fusion | flops 12607492 | bytes 4202512 | tf_op jit(solution)/shard_map/ks,cxysz->cxykz/dot_general | solution.py:88
  58.7 71.7 %collective-permute-done.1 = f32[19,24,24,48]{3,2,1,0:T(8,128)} collective-permute-done((f32[19,24,24,48]{3,2,1,0:T(8,128)}, f32[19,24,24,48]{3,2,1,0:T(8,128)}, u32[]{:S(2)}, u32[]{:S(2)}) %collective-permute-start.1) | collective-permute-done | bytes 2101280 | tf_op jit(solution)/shard_map/ppermute | solution.py:37
  130.4 11.2 %reshape.4302 = f32[19,24,24,2,24]{4,3,2,1,0:T(2,128)} reshape(f32[19,24,24,48]{3,2,1,0:T(8,128)} %collective-permute-done.1) | data formatting | bytes 4202496 | tf_op jit(solution)/shard_map/reshape | solution.py:104
  141.6 11.2 %reshape.4303 = f32[19,24,24,2,24]{4,3,2,1,0:T(2,128)} reshape(f32[19,24,24,48]{3,2,1,0:T(8,128)} %collective-permute-done.3) | data formatting | bytes 4202496 | tf_op jit(solution)/shard_map/reshape | solution.py:105
  152.8 35.5 %fusion.273 = f32[2,19,24,24,24]{4,0,3,2,1:T(2,128)} fusion(f32[19,24,24,2,24]{4,3,2,1,0:T(2,128)} %reshape.4302, s32[2]{0:T(128)S(1)} %collective-permute-done, s32[2]{0:T(128)S(1)} %iota_add_fusion), kind=kOutput, calls=%fused_computation.444 | convolution fusion | flops 12607492 | bytes 4202512 | tf_op jit(solution)/shard_map/ks,cxysz->cxykz/dot_general | solution.py:88
  188.3 32.2 %add_bitcast_fusion = f32[19,24,24,2,24]{4,3,2,1,0:T(2,128)} fusion(f32[2,19,24,24,24]{4,0,3,2,1:T(2,128)} %fusion.275, f32[2,19,24,24,24]{4,0,3,2,1:T(2,128)} %fusion.273, f32[19,24,24,2,24]{4,3,2,1,0:T(2,128)} %reshape.4303, s32[2]{0:T(128)S(1)} %collective-permute-done.2), kind=kOutput, calls=%fused_computation | convolution fusion | flops 13658116 | bytes 8405000 | tf_op jit(solution)/shard_map/ks,cxysz->cxykz/dot_general | solution.py:88
  220.5 8.2 %fusion.286 = (f32[1,24,24,2,24]{4,3,2,1,0:T(2,128)}, f32[1,24,24,2,24]{4,3,2,1,0:T(2,128)}, f32[1,24,24,2,24]{4,3,2,1,0:T(2,128)S(1)}, f32[1,24,24,2,24]{4,3,2,...) fusion(f32[19,24,24,2,24]{4,3,2,1,0:T(2,128)} %add_bitcast_fusion), kind=kLoop, calls=%fused_computation.459 | loop fusion | bytes 4202496 | tf_op jit(solution)/shard_map/slice | solution.py:68
  261.2 6.8 %collective-permute-start.4 = (f32[19,1,24,48]{3,2,1,0:T(8,128)S(1)}, f32[19,1,24,48]{3,2,1,0:T(8,128)S(1)}, u32[]{:S(2)}, u32[]{:S(2)}) collective-permute-start(f32[19,1,24,48]{3,2,1,0:T(8,128)S(1)} %get-tuple-element.65), channel_id=1, source_target_pairs={{16,0},{32,16},{48,32},{64,48},{80,64},{96,80},{112,96},{0,112},{1... | collective-permute-start | bytes 262664 | tf_op jit(solution)/shard_map/ppermute | solution.py:48
  268.4 3.0 collective-permute-done.4
  271.4 5.9 %collective-permute-done.5 = f32[19,1,24,48]{3,2,1,0:T(8,128)S(1)} collective-permute-done((f32[19,1,24,48]{3,2,1,0:T(8,128)S(1)}, f32[19,1,24,48]{3,2,1,0:T(8,128)S(1)}, u32[]{:S(2)}, u32[]{:S(2)}) %collective-permute-start.5) | collective-permute-done | bytes 87584 | tf_op jit(solution)/shard_map/ppermute | solution.py:47
  277.8 2.8 collective-permute-start.6
  280.7 5.7 %collective-permute-done.6 = f32[19,26,1,48]{3,2,1,0:T(1,128)S(1)} collective-permute-done((f32[19,26,1,48]{3,2,1,0:T(1,128)S(1)}, f32[19,26,1,48]{3,2,1,0:T(1,128)S(1)}, u32[]{:S(2)}, u32[]{:S(2)}) %collective-permute-start.6) | collective-permute-done | bytes 94880 | tf_op jit(solution)/shard_map/ppermute | solution.py:48
  286.5 3.4 pad_maximum_fusion
  289.9 7.1 %fusion.288 = (f32[19,26,26,1]{3,2,1,0:T(8,128)}, f32[19,26,26,1]{3,2,1,0:T(8,128)}) fusion(f32[19,26,26,48]{3,2,1,0:T(8,128)S(1)} %pad_maximum_fusion), kind=kLoop, calls=%fused_computation.461 | loop fusion | bytes 205504 | tf_op jit(solution)/shard_map/slice | solution.py:45
  297.0 6.0 %copy.213 = f32[19,26,26,1]{2,3,1,0:T(1,128)S(1)} copy(f32[19,26,26,1]{3,2,1,0:T(8,128)} %get-tuple-element.57) | data formatting | bytes 102752 | tf_op jit(solution)/shard_map/slice | solution.py:46
  303.7 6.0 %copy.215 = f32[19,26,26,1]{2,3,1,0:T(1,128)S(1)} copy(f32[19,26,26,1]{3,2,1,0:T(8,128)} %get-tuple-element.56) | data formatting | bytes 102752 | tf_op jit(solution)/shard_map/slice | solution.py:45
  312.5 5.7 %copy.214 = f32[19,26,26,1]{3,2,1,0:T(8,128)} copy(f32[19,26,26,1]{2,3,1,0:T(1,128)S(1)} %collective-permute-done.8) | data formatting | bytes 102752 | tf_op jit(solution)/shard_map/ppermute | solution.py:48
  318.3 5.7 %copy.216 = f32[19,26,26,1]{3,2,1,0:T(8,128)} copy(f32[19,26,26,1]{2,3,1,0:T(1,128)S(1)} %collective-permute-done.9) | data formatting | bytes 102752 | tf_op jit(solution)/shard_map/ppermute | solution.py:47
  324.0 7.7 %fusion.139 = (f32[19,24,24,48]{3,2,1,0:T(8,128)S(1)}, f32[1,24,24,48]{3,2,1,0:T(8,128)S(1)}, f32[1,24,24,48]{3,2,1,0:T(8,128)S(1)}, f32[1,24,24,48]{3,2,1,0:T(8...) fusion(f32[19,24,24,48]{3,2,1,0:T(8,128)} %copy-done.2, ...), kind=kLoop, calls=%fused_computation.182 | loop fusion | flops 4202495 | bytes 29528320
  336.1 5.1 %collective-permute-start.11 = (f32[19,1,24,48]{3,2,1,0:T(8,128)S(1)}, f32[19,1,24,48]{3,2,1,0:T(8,128)S(1)}, u32[]{:S(2)}, u32[]{:S(2)}) collective-permute-start(f32[19,1,24,48]{3,2,1,0:T(8,128)S(1)} %get-tuple-element.62), channel_id=1, source_target_pairs={{16,0},{32,16},{48,32},{64,48},{80,64},{96,80},{112,96},{0,112},{1... | collective-permute-start | bytes 262664 | tf_op jit(solution)/shard_map/ppermute | solution.py:48
  345.1 5.3 %collective-permute-start.12 = (f32[19,26,1,48]{3,2,1,0:T(1,128)S(1)}, f32[19,26,1,48]{3,2,1,0:T(1,128)S(1)}, u32[]{:S(2)}, u32[]{:S(2)}) collective-permute-start(f32[19,26,1,48]{3,2,1,0:T(1,128)S(1)} %get-tuple-element.59), channel_id=1, source_target_pairs={{0,4},{4,8},{8,12},{12,0},{1,5},{5,9},{9,13},{13,1},{2,6},{6,10},{... | collective-permute-start | bytes 284552 | tf_op jit(solution)/shard_map/ppermute | solution.py:47
  352.1 4.2 %collective-permute-done.12 = f32[19,26,1,48]{3,2,1,0:T(1,128)S(1)} collective-permute-done((f32[19,26,1,48]{3,2,1,0:T(1,128)S(1)}, f32[19,26,1,48]{3,2,1,0:T(1,128)S(1)}, u32[]{:S(2)}, u32[]{:S(2)}) %collective-permute-start.12) | collective-permute-done | bytes 94880 | tf_op jit(solution)/shard_map/ppermute | solution.py:47
  356.3 3.4 pad_maximum_fusion.1
  359.8 7.1 %fusion.287 = (f32[19,26,26,1]{3,2,1,0:T(8,128)}, f32[19,26,26,1]{3,2,1,0:T(8,128)}) fusion(f32[19,26,26,48]{3,2,1,0:T(8,128)S(1)} %pad_maximum_fusion.1), kind=kLoop, calls=%fused_computation.460 | loop fusion | bytes 205504 | tf_op jit(solution)/shard_map/slice | solution.py:46
  366.9 6.0 %copy.217 = f32[19,26,26,1]{2,3,1,0:T(1,128)S(1)} copy(f32[19,26,26,1]{3,2,1,0:T(8,128)} %get-tuple-element.55) | data formatting | bytes 102752 | tf_op jit(solution)/shard_map/slice | solution.py:45
  373.0 6.0 %copy.219 = f32[19,26,26,1]{2,3,1,0:T(1,128)S(1)} copy(f32[19,26,26,1]{3,2,1,0:T(8,128)} %get-tuple-element.54) | data formatting | bytes 102752 | tf_op jit(solution)/shard_map/slice | solution.py:46
  385.2 5.7 %copy.218 = f32[19,26,26,1]{3,2,1,0:T(8,128)} copy(f32[19,26,26,1]{2,3,1,0:T(1,128)S(1)} %collective-permute-done.14) | data formatting | bytes 102752 | tf_op jit(solution)/shard_map/ppermute | solution.py:47
  391.0 5.7 %copy.220 = f32[19,26,26,1]{3,2,1,0:T(8,128)} copy(f32[19,26,26,1]{2,3,1,0:T(1,128)S(1)} %collective-permute-done.15) | data formatting | bytes 102752 | tf_op jit(solution)/shard_map/ppermute | solution.py:48
  414.8 5.3 %reshape.4304 = f32[1,1,1,456,1152]{4,3,2,1,0:T(8,128)} reshape(f32[19,24,24,48]{3,2,1,0:T(8,128)} %fusion.266) | data formatting | bytes 4202496 | tf_op jit(solution)/shard_map/reshape | solution.py:111
  (166 shorter events, 75.5 us)
Async XLA Ops:
  0.0 12.7 %copy-start.3 = (f32[1,1,1,456,1152]{4,3,2,1,0:T(8,128)S(1)}, f32[1,1,1,456,1152]{4,3,2,1,0:T(8,128)}, u32[]{:S(2)}) copy-start(f32[1,1,1,456,1152]{4,3,2,1,0:T(8,128)} %param.3) | copy-start | bytes 6303748
  0.0 9.4 %copy-start.12 = (s32[2]{0:T(128)S(1)}, s32[2]{0:T(128)}, u32[]{:S(2)}) copy-start(s32[2]{0:T(128)} %param.4) | copy-start | bytes 28
  5.5 27.0 %copy-start.11 = (s32[1,1,1,24,1152]{4,3,2,1,0:T(8,128)S(1)}, s32[1,1,1,24,1152]{4,3,2,1,0:T(8,128)}, u32[]{:S(2)}) copy-start(s32[1,1,1,24,1152]{4,3,2,1,0:T(8,128)} %param.5) | copy-start | bytes 331780
  5.5 124.9 %collective-permute-start.1 = (f32[19,24,24,48]{3,2,1,0:T(8,128)}, f32[19,24,24,48]{3,2,1,0:T(8,128)}, u32[]{:S(2)}, u32[]{:S(2)}) collective-permute-start(f32[19,24,24,48]{3,2,1,0:T(8,128)} %reshape.4301), channel_id=1, source_target_pairs={{0,1},{1,2},{2,3},{3,4},{4,5},{5,6},{6,7},{7,8},{8,9},{9,10},{10,1... | collective-permute-start | bytes 6303752 | tf_op jit(solution)/shard_map/ppermute | solution.py:37
  7.5 134.1 %collective-permute-start.3 = (f32[19,24,24,48]{3,2,1,0:T(8,128)}, f32[19,24,24,48]{3,2,1,0:T(8,128)}, u32[]{:S(2)}, u32[]{:S(2)}) collective-permute-start(f32[19,24,24,48]{3,2,1,0:T(8,128)} %reshape.4301), channel_id=1, source_target_pairs={{0,127},{1,0},{2,1},{3,2},{4,3},{5,4},{6,5},{7,6},{8,7},{9,8},{10,... | collective-permute-start | bytes 6303752 | tf_op jit(solution)/shard_map/ppermute | solution.py:37
  9.4 143.4 %collective-permute-start = (s32[2]{0:T(128)S(1)}, s32[2]{0:T(128)S(1)}, u32[]{:S(2)}, u32[]{:S(2)}) collective-permute-start(s32[2]{0:T(128)S(1)} %copy-done.12), channel_id=1, source_target_pairs={{0,1},{1,2},{2,3},{3,4},{4,5},{5,6},{6,7},{7,8},{8,9},{9,10},{10,1... | collective-permute-start | bytes 32 | tf_op jit(solution)/shard_map/ppermute | solution.py:37
  9.4 178.9 %collective-permute-start.2 = (s32[2]{0:T(128)S(1)}, s32[2]{0:T(128)S(1)}, u32[]{:S(2)}, u32[]{:S(2)}) collective-permute-start(s32[2]{0:T(128)S(1)} %copy-done.12), channel_id=1, source_target_pairs={{0,127},{1,0},{2,1},{3,2},{4,3},{5,4},{6,5},{7,6},{8,7},{9,8},{10,... | collective-permute-start | bytes 32 | tf_op jit(solution)/shard_map/ppermute | solution.py:37
  254.1 2.6 copy-start.9
  254.1 2.9 copy-start.8
  257.4 1.0 copy-start.5
  257.8 1.0 copy-start.4
  261.1 28.8 %copy-start.2 = (f32[19,24,24,48]{3,2,1,0:T(8,128)}, f32[19,24,24,48]{3,2,1,0:T(8,128)S(1)}, u32[]{:S(2)}) copy-start(f32[19,24,24,48]{3,2,1,0:T(8,128)S(1)} %broadcast_select_fusion.1) | copy-start | bytes 6303748
  261.2 10.2 %collective-permute-start.4 = (f32[19,1,24,48]{3,2,1,0:T(8,128)S(1)}, f32[19,1,24,48]{3,2,1,0:T(8,128)S(1)}, u32[]{:S(2)}, u32[]{:S(2)}) collective-permute-start(f32[19,1,24,48]{3,2,1,0:T(8,128)S(1)} %get-tuple-element.65), channel_id=1, source_target_pairs={{16,0},{32,16},{48,32},{64,48},{80,64},{96,80},{112,96},{0,112},{1... | collective-permute-start | bytes 262664 | tf_op jit(solution)/shard_map/ppermute | solution.py:48
  268.0 9.4 %collective-permute-start.5 = (f32[19,1,24,48]{3,2,1,0:T(8,128)S(1)}, f32[19,1,24,48]{3,2,1,0:T(8,128)S(1)}, u32[]{:S(2)}, u32[]{:S(2)}) collective-permute-start(f32[19,1,24,48]{3,2,1,0:T(8,128)S(1)} %get-tuple-element.64), channel_id=1, source_target_pairs={{0,16},{16,32},{32,48},{48,64},{64,80},{80,96},{96,112},{112,0},{1... | collective-permute-start | bytes 262664 | tf_op jit(solution)/shard_map/ppermute | solution.py:47
  277.8 8.6 %collective-permute-start.6 = (f32[19,26,1,48]{3,2,1,0:T(1,128)S(1)}, f32[19,26,1,48]{3,2,1,0:T(1,128)S(1)}, u32[]{:S(2)}, u32[]{:S(2)}) collective-permute-start(f32[19,26,1,48]{3,2,1,0:T(1,128)S(1)} %get-tuple-element.61), channel_id=1, source_target_pairs={{4,0},{8,4},{12,8},{0,12},{5,1},{9,5},{13,9},{1,13},{6,2},{10,6},{... | collective-permute-start | bytes 284552 | tf_op jit(solution)/shard_map/ppermute | solution.py:48
  280.6 5.9 %collective-permute-start.7 = (f32[19,26,1,48]{3,2,1,0:T(1,128)S(1)}, f32[19,26,1,48]{3,2,1,0:T(1,128)S(1)}, u32[]{:S(2)}, u32[]{:S(2)}) collective-permute-start(f32[19,26,1,48]{3,2,1,0:T(1,128)S(1)} %get-tuple-element.60), channel_id=1, source_target_pairs={{0,4},{4,8},{8,12},{12,0},{1,5},{5,9},{9,13},{13,1},{2,6},{6,10},{... | collective-permute-start | bytes 284552 | tf_op jit(solution)/shard_map/ppermute | solution.py:47
  303.1 9.5 %collective-permute-start.8 = (f32[19,26,26,1]{2,3,1,0:T(1,128)S(1)}, f32[19,26,26,1]{2,3,1,0:T(1,128)S(1)}, u32[]{:S(2)}, u32[]{:S(2)}) collective-permute-start(f32[19,26,26,1]{2,3,1,0:T(1,128)S(1)} %copy.213), channel_id=1, source_target_pairs={{1,0},{2,1},{3,2},{0,3},{5,4},{6,5},{7,6},{4,7},{9,8},{10,9},{11,1... | collective-permute-start | bytes 154136 | tf_op jit(solution)/shard_map/ppermute | solution.py:48
  309.7 8.6 %collective-permute-start.9 = (f32[19,26,26,1]{2,3,1,0:T(1,128)S(1)}, f32[19,26,26,1]{2,3,1,0:T(1,128)S(1)}, u32[]{:S(2)}, u32[]{:S(2)}) collective-permute-start(f32[19,26,26,1]{2,3,1,0:T(1,128)S(1)} %copy.215), channel_id=1, source_target_pairs={{0,1},{1,2},{2,3},{3,0},{4,5},{5,6},{6,7},{7,4},{8,9},{9,10},{10,1... | collective-permute-start | bytes 154136 | tf_op jit(solution)/shard_map/ppermute | solution.py:47
  318.3 13.6 %slice-start.4 = ((s8[5603328]{0:T(1024)(128)(4,1)}), s8[1409024]{0:T(1024)(128)(4,1)S(1)}, s32[]{:S(2)}) async-start(s8[5603328]{0:T(1024)(128)(4,1)} %bitcast.36), calls=%async_computation.4 | async-start | bytes 2818048
  324.0 7.9 %slice-start.5 = ((s8[5603328]{0:T(1024)(128)(4,1)}), s8[4194304]{0:T(1024)(128)(4,1)S(1)}, s32[]{:S(2)}) async-start(s8[5603328]{0:T(1024)(128)(4,1)} %bitcast.36), calls=%async_computation.5 | async-start | bytes 8388608
  336.0 20.4 %copy-start = (f32[19,24,24,48]{3,2,1,0:T(8,128)}, f32[19,24,24,48]{3,2,1,0:T(8,128)S(1)}, u32[]{:S(2)}) copy-start(f32[19,24,24,48]{3,2,1,0:T(8,128)S(1)} %broadcast_select_fusion) | copy-start | bytes 6303748
  336.0 8.6 %collective-permute-start.10 = (f32[19,1,24,48]{3,2,1,0:T(8,128)S(1)}, f32[19,1,24,48]{3,2,1,0:T(8,128)S(1)}, u32[]{:S(2)}, u32[]{:S(2)}) collective-permute-start(f32[19,1,24,48]{3,2,1,0:T(8,128)S(1)} %get-tuple-element.63), channel_id=1, source_target_pairs={{0,16},{16,32},{32,48},{48,64},{64,80},{80,96},{96,112},{112,0},{1... | collective-permute-start | bytes 262664 | tf_op jit(solution)/shard_map/ppermute | solution.py:47
  336.1 8.5 %collective-permute-start.11 = (f32[19,1,24,48]{3,2,1,0:T(8,128)S(1)}, f32[19,1,24,48]{3,2,1,0:T(8,128)S(1)}, u32[]{:S(2)}, u32[]{:S(2)}) collective-permute-start(f32[19,1,24,48]{3,2,1,0:T(8,128)S(1)} %get-tuple-element.62), channel_id=1, source_target_pairs={{16,0},{32,16},{48,32},{64,48},{80,64},{96,80},{112,96},{0,112},{1... | collective-permute-start | bytes 262664 | tf_op jit(solution)/shard_map/ppermute | solution.py:48
  345.1 11.3 %collective-permute-start.12 = (f32[19,26,1,48]{3,2,1,0:T(1,128)S(1)}, f32[19,26,1,48]{3,2,1,0:T(1,128)S(1)}, u32[]{:S(2)}, u32[]{:S(2)}) collective-permute-start(f32[19,26,1,48]{3,2,1,0:T(1,128)S(1)} %get-tuple-element.59), channel_id=1, source_target_pairs={{0,4},{4,8},{8,12},{12,0},{1,5},{5,9},{9,13},{13,1},{2,6},{6,10},{... | collective-permute-start | bytes 284552 | tf_op jit(solution)/shard_map/ppermute | solution.py:47
  350.4 5.9 %collective-permute-start.13 = (f32[19,26,1,48]{3,2,1,0:T(1,128)S(1)}, f32[19,26,1,48]{3,2,1,0:T(1,128)S(1)}, u32[]{:S(2)}, u32[]{:S(2)}) collective-permute-start(f32[19,26,1,48]{3,2,1,0:T(1,128)S(1)} %get-tuple-element.58), channel_id=1, source_target_pairs={{4,0},{8,4},{12,8},{0,12},{5,1},{9,5},{13,9},{1,13},{6,2},{10,6},{... | collective-permute-start | bytes 284552 | tf_op jit(solution)/shard_map/ppermute | solution.py:48
  372.9 12.3 %collective-permute-start.14 = (f32[19,26,26,1]{2,3,1,0:T(1,128)S(1)}, f32[19,26,26,1]{2,3,1,0:T(1,128)S(1)}, u32[]{:S(2)}, u32[]{:S(2)}) collective-permute-start(f32[19,26,26,1]{2,3,1,0:T(1,128)S(1)} %copy.217), channel_id=1, source_target_pairs={{0,1},{1,2},{2,3},{3,0},{4,5},{5,6},{6,7},{7,4},{8,9},{9,10},{10,1... | collective-permute-start | bytes 154136 | tf_op jit(solution)/shard_map/ppermute | solution.py:47
  379.0 11.9 %collective-permute-start.15 = (f32[19,26,26,1]{2,3,1,0:T(1,128)S(1)}, f32[19,26,26,1]{2,3,1,0:T(1,128)S(1)}, u32[]{:S(2)}, u32[]{:S(2)}) collective-permute-start(f32[19,26,26,1]{2,3,1,0:T(1,128)S(1)} %copy.219), channel_id=1, source_target_pairs={{1,0},{2,1},{3,2},{0,3},{5,4},{6,5},{7,6},{4,7},{9,8},{10,9},{11,1... | collective-permute-start | bytes 154136 | tf_op jit(solution)/shard_map/ppermute | solution.py:48
  391.0 7.9 %slice-start = ((s8[5603328]{0:T(1024)(128)(4,1)}), s8[1409024]{0:T(1024)(128)(4,1)S(1)}, s32[]{:S(2)}) async-start(s8[5603328]{0:T(1024)(128)(4,1)} %bitcast.32), calls=%async_computation | async-start | bytes 2818048
  396.7 2.5 slice-start.1
  396.7 4.9 %copy-start.1 = (f32[19,26,26,1]{3,2,1,0:T(8,128)S(1)}, f32[19,26,26,1]{3,2,1,0:T(8,128)}, u32[]{:S(2)}) copy-start(f32[19,26,26,1]{3,2,1,0:T(8,128)} %copy.220) | copy-start | bytes 154132
  403.4 2.4 slice-start.2
  404.2 3.1 slice-start.3
  (3 other events, 2.8 us)
where the time goes:
time: 425 us; the launch traced here: 420 us
  local copies, waits for them, and re-layouts  156 us (37%)
  waiting for transfers between devices  93.4 us (22%)
  matrix products  93.1 us (22%)
  other arithmetic  44.3 us (10%)
  starting transfers between devices  32.5 us (8%)
    dot_general x3, matrix products, select(): jnp.einsum('ks,cxysz->cxykz', table, blocks, precision=lax.Precision.HIGH...  93.1 us
    ppermute x4, waiting for transfers between devices, from_behind(): lax.ppermute(shard, axis, [(i, (i + by) % devices) for i in range(devices)])  71.7 us
    unnamed x56, other arithmetic  33.6 us
    slice x20, local copies, waits for them, and re-layouts, collide(): bounced = jnp.stack([f[o] for o in OPPOSITE])  33.5 us
    another operation x1, local copies, waits for them, and re-layouts, per_device(): blocks = cells.reshape(19, edge, edge, count, edge)  19.8 us
    slice x4, local copies, waits for them, and re-layouts, extended(): initial = lax.slice_in_dim(shard, 0, width, axis=dim)  19.2 us
    slice x4, local copies, waits for them, and re-layouts, extended(): last = lax.slice_in_dim(shard, length - width, length, axis=dim)  19.2 us
    ppermute x6, starting transfers between devices, extended(): after = lax.ppermute(initial, axis, down)  18.2 us
  transfers between devices with their start and end apart: 16, of which 7 were waited for; matrix products, arithmetic and copies ran while one was open for 32% of the time, Pallas kernels for 0%

commit v1 on v0

v1 whole, which is shorter than its diff:
```python
import functools

import jax
import jax.numpy as jnp
from jax import lax
from jax.experimental import pallas as pl
from jax.experimental.pallas import tpu as pltpu
from jax.sharding import PartitionSpec as P

STEPS = 2
VELS = [
    (0, 0, 0),
    (1, 0, 0),
    (-1, 0, 0),
    (0, 1, 0),
    (0, -1, 0),
    (0, 0, 1),
    (0, 0, -1),
    (1, 1, 0),
    (-1, -1, 0),
    (1, -1, 0),
    (-1, 1, 0),
    (1, 0, 1),
    (-1, 0, -1),
    (1, 0, -1),
    (-1, 0, 1),
    (0, 1, 1),
    (0, -1, -1),
    (0, 1, -1),
    (0, -1, 1),
]
WEIGHTS = [1.0 / 3.0] + [1.0 / 18.0] * 6 + [1.0 / 36.0] * 12
OPPOSITE = [VELS.index((-a, -b, -c)) for a, b, c in VELS]
OMEGA = 1.25
MESH = pl.DeviceIdType.MESH
DIRS = VELS[1:]
BS = 24
ROW = 2 * BS
LANES = BS * ROW
TILES = BS // 8
COLS = LANES // 128
PACKED = 9 * TILES + 2


def with_component(axis, sign):
    return [i for i, c in enumerate(VELS) if c[axis] == sign]


def place_of(delta):
    sx, sy, sz = (lax.axis_size(a) for a in ("gx", "gy", "gz"))
    x, y, z = (lax.axis_index(a) for a in ("gx", "gy", "gz"))
    total = sx * sy * sz
    p = lax.rem((x * sy + y) * sz + z + (delta + total), total)
    return (p // (sy * sz), lax.rem(p // sz, sy), lax.rem(p, sz))


def beside(c):
    place = []
    for axis, by in zip(("gx", "gy", "gz"), c):
        size = lax.axis_size(axis)
        place.append(lax.rem(lax.axis_index(axis) + (by + size), size))
    return tuple(place)


def collide(f, solid):
    rho = functools.reduce(lambda a, b: a + b, f)
    inv = 1.0 / rho
    vel = []
    for axis in range(3):
        plus = [f[i] for i in with_component(axis, 1)]
        minus = [f[i] for i in with_component(axis, -1)]
        vel.append((sum(plus[1:], plus[0]) - sum(minus[1:], minus[0])) * inv)
    speed = vel[0] * vel[0] + vel[1] * vel[1] + vel[2] * vel[2]
    base = 1.0 - 1.5 * speed
    bounce = solid == 1
    posts = [None] * 19
    weighted = {w: (OMEGA * w) * rho for w in set(WEIGHTS)}
    for i in range(19):
        if posts[i] is not None:
            continue
        o = OPPOSITE[i]
        w = weighted[WEIGHTS[i]]
        if i == o:
            posts[i] = jnp.where(bounce, f[i], (1.0 - OMEGA) * f[i] + w * base)
            continue
        along = None
        for axis in range(3):
            if VELS[i][axis] == 1:
                along = vel[axis] if along is None else along + vel[axis]
            elif VELS[i][axis] == -1:
                along = -vel[axis] if along is None else along - vel[axis]
        even = w * (base + 4.5 * (along * along))
        odd = (3.0 * w) * along
        posts[i] = jnp.where(bounce, f[o], (1.0 - OMEGA) * f[i] + (even + odd))
        posts[o] = jnp.where(bounce, f[i], (1.0 - OMEGA) * f[o] + (even - odd))
    return posts


def kernel(
    codes, popul, solid, fields,
    cells, home, post, send_up, send_down, got_up, got_down,
    faces_x, faces_y, faces_z, got_x, got_y, got_z, got_xy, got_xz, got_yz,
    load_sem, ring_send, ring_recv, halo_send, halo_recv,
):
    load = pltpu.make_async_copy(popul, cells, load_sem)
    load.start()
    following, previous = place_of(1), place_of(-1)
    partners = [following, previous] + [beside(c) for c in DIRS]
    barrier = pltpu.get_barrier_semaphore()
    for partner in partners:
        pl.semaphore_signal(barrier, inc=1, device_id=partner, device_id_type=MESH)

    lane = lax.broadcasted_iota(jnp.int32, (8, LANES), 1)
    z = lax.rem(lane, ROW)
    first = z < BS
    ordered = jnp.broadcast_to(codes[1], (8, LANES)) >= 3
    from_low = first & (jnp.broadcast_to(jnp.minimum(codes[0], codes[1]), (8, LANES)) == 1)
    from_high = jnp.logical_not(first) & (
        jnp.broadcast_to(jnp.maximum(codes[0], codes[1]), (8, LANES)) == 4
    )
    load.wait()

    def both_orders(i, t):
        a = cells[i, 8 * t : 8 * t + 8, :]
        w = jnp.where(first, pltpu.roll(a, LANES - BS, 1), pltpu.roll(a, BS, 1))
        normal = jnp.where(ordered, a, w)
        home[i, 8 * t : 8 * t + 8, :] = normal
        return normal, jnp.where(ordered, w, a)

    def pairs():
        for t in range(TILES):
            for k in range(9):
                yield 9 * t + k, (2 * k, t), (2 * k + 1, t)
        yield 9 * TILES, (18, 0), (18, 1)
        yield 9 * TILES + 1, (18, 2), None

    for row, one, two in pairs():
        normal_one, swapped_one = both_orders(*one)
        normal_two, swapped_two = (normal_one, swapped_one) if two is None else both_orders(*two)
        send_up[row] = jnp.where(first, swapped_one, normal_two)
        send_down[row] = jnp.where(first, normal_one, swapped_two)

    pl.semaphore_wait(barrier, len(partners))
    ring = []
    for way, (source, target, device) in enumerate(
        ((send_up, got_up, following), (send_down, got_down, previous))
    ):
        copy = pltpu.make_async_remote_copy(
            src_ref=source,
            dst_ref=target,
            send_sem=ring_send.at[way],
            recv_sem=ring_recv.at[way],
            device_id=device,
            device_id_type=MESH,
        )
        copy.start()
        ring.append(copy)
    for copy in ring:
        copy.wait()

    for row, one, two in pairs():
        low, high = got_up[row], got_down[row]
        i, t = one
        here = slice(8 * t, 8 * t + 8)
        own = jnp.where(from_low, low, home[i, here, :])
        home[i, here, :] = jnp.where(from_high, pltpu.roll(high, BS, 1), own)
        if two is not None:
            i, t = two
            here = slice(8 * t, 8 * t + 8)
            own = jnp.where(from_low, pltpu.roll(low, LANES - BS, 1), home[i, here, :])
            home[i, here, :] = jnp.where(from_high, high, own)

    row_at = lax.broadcasted_iota(jnp.int32, (BS, LANES), 0)
    lane_at = lax.broadcasted_iota(jnp.int32, (BS, LANES), 1)
    z_at = lax.rem(lane_at, ROW)
    for step in range(STEPS):

        def one_tile(n, carry):
            t, j = n // COLS, lax.rem(n, COLS)
            rows = pl.ds(pl.multiple_of(t * 8, 8), 8)
            cols = pl.ds(pl.multiple_of(j * 128, 128), 128)
            posts = collide([home[i, rows, cols] for i in range(19)], solid[rows, cols])
            for i in range(19):
                post[i, rows, cols] = posts[i]
            return carry

        lax.fori_loop(0, TILES * COLS, one_tile, 0)

        copies = []

        def send(c, source, target):
            n = DIRS.index(c)
            copy = pltpu.make_async_remote_copy(
                src_ref=source,
                dst_ref=target,
                send_sem=halo_send.at[step, n],
                recv_sem=halo_recv.at[step, n],
                device_id=beside(c),
                device_id_type=MESH,
            )
            copy.start()
            copies.append(copy)

        for side, sign in enumerate((1, -1)):
            out_z = ROW - 1 if sign == 1 else 0
            packed = None
            for k, i in enumerate(with_component(2, sign)):
                for t in range(TILES):
                    q = TILES * k + t
                    part = post[i, 8 * t : 8 * t + 8, :]
                    part = pltpu.roll(part, (-sign * q) % LANES, 1) if q else part
                    packed = part if packed is None else jnp.where(z == out_z - sign * q, part, packed)
            faces_z[step, side] = packed
            send((0, 0, sign), faces_z.at[step, side], got_z.at[step, side])
        for side, sign in enumerate((1, -1)):
            exit_x = BS - 1 if sign == 1 else 0
            for k, i in enumerate(with_component(0, sign)):
                faces_x[step, side, k : k + 1, :] = post[i, exit_x : exit_x + 1, :]
            send((sign, 0, 0), faces_x.at[step, side], got_x.at[step, side])
        for side, sign in enumerate((1, -1)):
            at = LANES - 128 if sign == 1 else 0
            for k, i in enumerate(with_component(1, sign)):
                faces_y[step, side, k] = post[i, :, at : at + 128]
            send((0, sign, 0), faces_y.at[step, side], got_y.at[step, side])
        for i in range(7, 19):
            cx, cy, cz = VELS[i]
            rows = slice(BS - 8, BS) if cx == 1 else slice(0, 8)
            cols = slice(LANES - 128, LANES) if cy == 1 else slice(0, 128)
            if cz == 0:
                send(VELS[i], post.at[i, rows, cols], got_xy.at[step, i - 7])
            elif cy == 0:
                send(VELS[i], post.at[i, rows, :], got_xz.at[step, i - 11])
            else:
                send(VELS[i], post.at[i, :, cols], got_yz.at[step, i - 15])
        for copy in copies:
            copy.wait()

        target = fields if step == STEPS - 1 else home
        for i in range(19):
            cx, cy, cz = VELS[i]
            v = post[i]
            out_z = ROW - 1 if cz == 1 else 0
            at_y = lane_at >= LANES - ROW if cy == 1 else lane_at < ROW
            at_x = row_at == (BS - 1 if cx == 1 else 0)
            at_z = z_at == out_z
            side_x, side_y, side_z = (0 if c == 1 else 1 for c in (cx, cy, cz))
            shift_z = -cz * ROW

            def widened(tile):
                rest = jnp.zeros((tile.shape[0], LANES - 128), jnp.float32)
                return jnp.concatenate([rest, tile] if cy == 1 else [tile, rest], axis=1)

            if cz:
                k = with_component(2, cz).index(i)
                packed = got_z[step, side_z]
                parts = [
                    pltpu.roll(packed, (cz * (TILES * k + t) + shift_z) % LANES, 1)
                    for t in range(TILES)
                ]
                v = jnp.where(at_z, jnp.concatenate(parts, axis=0), v)
            if cy:
                k = with_component(1, cy).index(i)
                inside = at_y & jnp.logical_not(at_z) if cz else at_y
                v = jnp.where(inside, widened(got_y[step, side_y, k]), v)
            if cy and cz:
                edge = pltpu.roll(widened(got_yz[step, i - 15]), shift_z % LANES, 1)
                slot_y = ((BS - 1 if cy == 1 else 0) - cz) % BS
                v = jnp.where(lane_at == slot_y * ROW + out_z, edge, v)
            if cx:
                k = with_component(0, cx).index(i)
                row = jnp.broadcast_to(got_x[step, side_x, k : k + 1, :], (BS, LANES))
                if cy:
                    r = 7 if cx == 1 else 0
                    edge = widened(got_xy[step, i - 7, r : r + 1, :])
                    row = jnp.where(at_y, jnp.broadcast_to(edge, (BS, LANES)), row)
                if cz:
                    r = 7 if cx == 1 else 0
                    edge = pltpu.roll(got_xz[step, i - 11], shift_z % LANES, 1)[r : r + 1, :]
                    row = jnp.where(at_z, jnp.broadcast_to(edge, (BS, LANES)), row)
                v = jnp.where(at_x, row, v)
            if cx:
                v = pltpu.roll(v, cx % BS, 0)
            if cy or cz:
                v = pltpu.roll(v, (cy * ROW + cz) % LANES, 1)
            target[i] = v


def per_device(popul, codes, solid):
    vmem = pl.BlockSpec(memory_space=pltpu.VMEM)
    fields = pl.pallas_call(
        kernel,
        out_shape=jax.ShapeDtypeStruct((19, BS, LANES), jnp.float32),
        in_specs=[
            pl.BlockSpec(memory_space=pltpu.SMEM),
            pl.BlockSpec(memory_space=pl.ANY),
            vmem,
        ],
        out_specs=vmem,
        scratch_shapes=[
            pltpu.VMEM((19, BS, LANES), jnp.float32),
            pltpu.VMEM((19, BS, LANES), jnp.float32),
            pltpu.VMEM((19, BS, LANES), jnp.float32),
            pltpu.VMEM((PACKED, 8, LANES), jnp.float32),
            pltpu.VMEM((PACKED, 8, LANES), jnp.float32),
            pltpu.VMEM((PACKED, 8, LANES), jnp.float32),
            pltpu.VMEM((PACKED, 8, LANES), jnp.float32),
            pltpu.VMEM((STEPS, 2, 8, LANES), jnp.float32),
            pltpu.VMEM((STEPS, 2, 5, BS, 128), jnp.float32),
            pltpu.VMEM((STEPS, 2, 8, LANES), jnp.float32),
            pltpu.VMEM((STEPS, 2, 8, LANES), jnp.float32),
            pltpu.VMEM((STEPS, 2, 5, BS, 128), jnp.float32),
            pltpu.VMEM((STEPS, 2, 8, LANES), jnp.float32),
            pltpu.VMEM((STEPS, 4, 8, 128), jnp.float32),
            pltpu.VMEM((STEPS, 4, 8, LANES), jnp.float32),
            pltpu.VMEM((STEPS, 4, BS, 128), jnp.float32),
            pltpu.SemaphoreType.DMA,
            pltpu.SemaphoreType.DMA((2,)),
            pltpu.SemaphoreType.DMA((2,)),
            pltpu.SemaphoreType.DMA((STEPS, 18)),
            pltpu.SemaphoreType.DMA((STEPS, 18)),
        ],
        compiler_params=pltpu.CompilerParams(
            collective_id=0, has_side_effects=True, vmem_limit_bytes=48 * 1024 * 1024
        ),
        cost_estimate=pl.CostEstimate(flops=14_000_000, bytes_accessed=4_500_000, transcendentals=0),
    )(codes, popul.reshape(19, BS, LANES), solid.reshape(BS, LANES))
    return fields.reshape(popul.shape)


def solution(mesh):
    placed = (
        P("gx", "gy", "gz", None, None),
        P(("gx", "gy", "gz")),
        P("gx", "gy", "gz", None, None),
    )
    return jax.shard_map(
        per_device,
        mesh=mesh,
        in_specs=placed,
        out_specs=P("gx", "gy", "gz", None, None),
        check_vma=False,
    )
```

time: 425 us -> 63.6 us (0.15); the launches traced: 420 us -> 63.4 us
  local copies, waits for them, and re-layouts: 156 us -> 4.47 us
  waiting for transfers between devices: 93.4 us -> 0 us
  matrix products: 93.1 us -> 0 us
  Pallas kernels: 0 us -> 59 us
  other arithmetic: 44.3 us -> 0 us
  starting transfers between devices: 32.5 us -> 0 us
    ppermute x16 -> x0, waiting for transfers between devices: 93.4 us -> none  [the longest x4 71.7 us: from_behind(): lax.ppermute(shard, axis, [(i, (i + by) % devices) for i in range(devices)])]
    dot_general x3 -> x0, matrix products: 93.1 us -> none  [select(): jnp.einsum('ks,cxysz->cxykz', table, blocks, precision=lax.Precision.HIGH...]
    slice x28 -> x0, local copies, waits for them, and re-layouts: 71.9 us -> none  [the longest x20 33.5 us: collide(): bounced = jnp.stack([f[o] for o in OPPOSITE])]
    pallas_call x0 -> x1, Pallas kernels: none -> 59 us  [per_device(): pl.pallas_call(kernel, out_shape=jax.ShapeDtypeStruct((19, BS, LANES), jn...]
    unnamed x56 -> x0, other arithmetic: 33.6 us -> none
    reshape x4 -> x0, local copies, waits for them, and re-layouts: 33.1 us -> none  [the longest x1 11.2 us: per_device(): lower_pop.reshape(19, edge, edge, count, edge)]
    ppermute x16 -> x0, starting transfers between devices: 32.5 us -> none  [the longest x6 18.2 us: extended(): after = lax.ppermute(initial, axis, down)]
    ppermute x4 -> x0, local copies, waits for them, and re-layouts: 23 us -> none  [the longest x2 11.5 us: extended(): after = lax.ppermute(initial, axis, down)]
  transfers between devices with their start and end apart: 16 -> 0, of which waited for: 7 -> 0; matrix products, arithmetic and copies ran while one was open for 32% -> 0% of each run, Pallas kernels for 0% -> 0%
where the time goes in v1:
time: 63.6 us; the launch traced here: 63.4 us
  Pallas kernels  59 us (93%)
  local copies, waits for them, and re-layouts  4.47 us (7%)
    pallas_call x1, Pallas kernels, per_device(): pl.pallas_call(kernel, out_shape=jax.ShapeDtypeStruct((19, BS, LANES), jn...  59 us
    unnamed x7, local copies, waits for them, and re-layouts  4.47 us

profile of v1, /device:TPU:1, one launch (start us, length us, event | category | flops | bytes accessed | tf_op | source)
XLA Modules:
  0.0 63.4 jit_solution(3017407702840495992)
XLA Ops:
  0.0 0.0 copy-start
  0.0 1.6 %copy-done = f32[1,1,1,456,1152]{4,3,2,1,0:T(8,128)S(1)} copy-done((f32[1,1,1,456,1152]{4,3,2,1,0:T(8,128)S(1)}, f32[1,1,1,456,1152]{4,3,2,1,0:T(8,128)}, u32[]{:S(2)}) %copy-start) | copy-done | bytes 2101272
  1.6 0.0 copy-start.1
  1.6 0.9 %copy-done.1 = s32[1,1,1,24,1152]{4,3,2,1,0:T(8,128)S(1)} copy-done((s32[1,1,1,24,1152]{4,3,2,1,0:T(8,128)S(1)}, s32[1,1,1,24,1152]{4,3,2,1,0:T(8,128)}, u32[]{:S(2)}) %copy-start.1) | copy-done | bytes 110616
  2.5 0.0 copy-start.2
  2.5 0.7 %copy-done.2 = s32[2]{0:T(128)S(1)} copy-done((s32[2]{0:T(128)S(1)}, s32[2]{0:T(128)}, u32[]{:S(2)}) %copy-start.2) | copy-done | bytes 32
  3.1 59.0 %shard_map.37 = f32[19,24,1152]{2,1,0:T(8,128)S(1)} custom-call(s32[2]{0:T(128)S(1)} %copy-done.2, f32[19,24,1152]{2,1,0:T(8,128)S(1)} %bitcast.4, s32[24,1152]{1,0:T(8,128)S(1)} %bitcast.5), custom_call_target="tpu_custom_call" | custom-call | flops 14000000 | bytes 4500000 | tf_op jit(solution)/shard_map/pallas_call | solution.py:290
  62.1 1.3 %copy.5 = f32[1,1,1,456,1152]{4,3,2,1,0:T(8,128)} copy(f32[1,1,1,456,1152]{4,3,2,1,0:T(8,128)S(1)} %bitcast.3) | data formatting | bytes 4202496
Async XLA Ops:
  0.0 1.6 %copy-start = (f32[1,1,1,456,1152]{4,3,2,1,0:T(8,128)S(1)}, f32[1,1,1,456,1152]{4,3,2,1,0:T(8,128)}, u32[]{:S(2)}) copy-start(f32[1,1,1,456,1152]{4,3,2,1,0:T(8,128)} %param.3) | copy-start | bytes 6303748
  1.6 0.9 %copy-start.1 = (s32[1,1,1,24,1152]{4,3,2,1,0:T(8,128)S(1)}, s32[1,1,1,24,1152]{4,3,2,1,0:T(8,128)}, u32[]{:S(2)}) copy-start(s32[1,1,1,24,1152]{4,3,2,1,0:T(8,128)} %param.5) | copy-start | bytes 331780
  2.5 0.7 %copy-start.2 = (s32[2]{0:T(128)S(1)}, s32[2]{0:T(128)}, u32[]{:S(2)}) copy-start(s32[2]{0:T(128)} %codes.1) | copy-start | bytes 28

commit v2 on v0

v2 whole, which is shorter than its diff:
```python
import functools

import jax
import jax.numpy as jnp
from jax import lax
from jax.experimental import pallas as pl
from jax.experimental.pallas import tpu as pltpu
from jax.sharding import PartitionSpec as P

STEPS = 2
VELS = [
    (0, 0, 0),
    (1, 0, 0),
    (-1, 0, 0),
    (0, 1, 0),
    (0, -1, 0),
    (0, 0, 1),
    (0, 0, -1),
    (1, 1, 0),
    (-1, -1, 0),
    (1, -1, 0),
    (-1, 1, 0),
    (1, 0, 1),
    (-1, 0, -1),
    (1, 0, -1),
    (-1, 0, 1),
    (0, 1, 1),
    (0, -1, -1),
    (0, 1, -1),
    (0, -1, 1),
]
WEIGHTS = [1.0 / 3.0] + [1.0 / 18.0] * 6 + [1.0 / 36.0] * 12
OPPOSITE = [VELS.index((-a, -b, -c)) for a, b, c in VELS]
OMEGA = 1.25
MESH = pl.DeviceIdType.MESH
DIRS = VELS[1:]
BS = 24
ROW = 2 * BS
LANES = BS * ROW
TILES = BS // 8
COLS = LANES // 128
THIRD = LANES // 3
PAD = 8
SPOT = {0: 0, 2: 8, 1: 16}
FIRST_ROW = {0: 2, 2: 11, 1: 20}
PACKED = 29


def with_component(axis, sign):
    return [i for i, c in enumerate(VELS) if c[axis] == sign]


def place_of(delta):
    sx, sy, sz = (lax.axis_size(a) for a in ("gx", "gy", "gz"))
    x, y, z = (lax.axis_index(a) for a in ("gx", "gy", "gz"))
    total = sx * sy * sz
    p = lax.rem((x * sy + y) * sz + z + (delta + total), total)
    return (p // (sy * sz), lax.rem(p // sz, sy), lax.rem(p, sz))


def beside(c):
    place = []
    for axis, by in zip(("gx", "gy", "gz"), c):
        size = lax.axis_size(axis)
        place.append(lax.rem(lax.axis_index(axis) + (by + size), size))
    return tuple(place)


def collide(f, solid):
    rho = functools.reduce(lambda a, b: a + b, f)
    inv = 1.0 / rho
    vel = []
    for axis in range(3):
        plus = [f[i] for i in with_component(axis, 1)]
        minus = [f[i] for i in with_component(axis, -1)]
        vel.append((sum(plus[1:], plus[0]) - sum(minus[1:], minus[0])) * inv)
    speed = vel[0] * vel[0] + vel[1] * vel[1] + vel[2] * vel[2]
    base = 1.0 - 1.5 * speed
    bounce = solid == 1
    posts = [None] * 19
    weighted = {w: (OMEGA * w) * rho for w in set(WEIGHTS)}
    for i in range(19):
        if posts[i] is not None:
            continue
        o = OPPOSITE[i]
        w = weighted[WEIGHTS[i]]
        if i == o:
            posts[i] = jnp.where(bounce, f[i], (1.0 - OMEGA) * f[i] + w * base)
            continue
        along = None
        for axis in range(3):
            if VELS[i][axis] == 1:
                along = vel[axis] if along is None else along + vel[axis]
            elif VELS[i][axis] == -1:
                along = -vel[axis] if along is None else along - vel[axis]
        even = w * (base + 4.5 * (along * along))
        odd = (3.0 * w) * along
        posts[i] = jnp.where(bounce, f[o], (1.0 - OMEGA) * f[i] + (even + odd))
        posts[o] = jnp.where(bounce, f[i], (1.0 - OMEGA) * f[o] + (even - odd))
    return posts


def kernel(
    held_codes, popul, held_solid, fields,
    codes, solid, cells, home, flow, post, send_up, send_down, got_up, got_down,
    out_x, out_y, out_z, out_yz, got_x, got_y, got_z, got_yz, got_xy, got_xz,
    load_sem, ring_send, ring_recv, halo_send, halo_recv,
):
    def rows_of(t):
        return slice(8 * t, 8 * t + 8)

    def padded(t, by=0):
        return slice(PAD + 8 * t + by, PAD + 8 * t + 8 + by)

    sources = [
        (held_codes, codes),
        (popul.at[18], cells.at[18]),
        (popul.at[0:18, rows_of(0)], cells.at[0:18, rows_of(0)]),
        (popul.at[0:18, rows_of(2)], cells.at[0:18, rows_of(2)]),
        (popul.at[0:18, rows_of(1)], cells.at[0:18, rows_of(1)]),
        (held_solid, solid),
    ]
    loads = [
        pltpu.make_async_copy(source, target, load_sem.at[n])
        for n, (source, target) in enumerate(sources)
    ]
    for load in loads:
        load.start()
    following, previous = place_of(1), place_of(-1)
    partners = [following, previous] + [beside(c) for c in DIRS]
    barrier = pltpu.get_barrier_semaphore()
    for partner in partners:
        pl.semaphore_signal(barrier, inc=1, device_id=partner, device_id_type=MESH)

    lane = lax.broadcasted_iota(jnp.int32, (8, LANES), 1)
    z = lax.rem(lane, ROW)
    z_third = z[:, :THIRD]
    first = z < BS
    loads[0].wait()
    low_code = jnp.minimum(codes[0], codes[1])
    high_code = jnp.maximum(codes[0], codes[1])
    ordered = jnp.broadcast_to(codes[1], (8, LANES)) >= 3
    from_low = first & (jnp.broadcast_to(low_code, (8, LANES)) == 1)
    from_high = jnp.logical_not(first) & (jnp.broadcast_to(high_code, (8, LANES)) == 4)

    def both_orders(i, t):
        a = cells[i, rows_of(t), :]
        w = jnp.where(first, pltpu.roll(a, LANES - BS, 1), pltpu.roll(a, BS, 1))
        normal = jnp.where(ordered, a, w)
        home[i, rows_of(t), :] = normal
        return normal, jnp.where(ordered, w, a)

    def pack(row, one, two):
        normal_one, swapped_one = both_orders(*one)
        normal_two, swapped_two = (normal_one, swapped_one) if two is None else both_orders(*two)
        send_up[row] = jnp.where(first, swapped_one, normal_two)
        send_down[row] = jnp.where(first, normal_one, swapped_two)

    def pack_tile(t):
        for k in range(9):
            pack(FIRST_ROW[t] + k, (2 * k, t), (2 * k + 1, t))

    ring = {}

    def send_ring(n, rows, planes):
        pair = []
        for way, (source, target, device) in enumerate(
            ((send_up, got_up, following), (send_down, got_down, previous))
        ):
            copy = pltpu.make_async_remote_copy(
                src_ref=source.at[rows, planes, :],
                dst_ref=target.at[rows, planes, :],
                send_sem=ring_send.at[way, n],
                recv_sem=ring_recv.at[way, n],
                device_id=device,
                device_id_type=MESH,
            )
            copy.start()
            pair.append(copy)
        ring[n] = pair

    def await_ring(n):
        for copy in ring[n]:
            copy.wait_recv()

    def unpack(row, one, two, planes=slice(0, 8)):
        low, high = got_up[row, planes, :], got_down[row, planes, :]
        i, t = one
        here = slice(8 * t + planes.start, 8 * t + planes.stop)
        own = jnp.where(from_low[planes], low, home[i, here, :])
        home[i, here, :] = jnp.where(from_high[planes], pltpu.roll(high, BS, 1), own)
        if two is not None:
            i, t = two
            here = slice(8 * t + planes.start, 8 * t + planes.stop)
            own = jnp.where(from_low[planes], pltpu.roll(low, LANES - BS, 1), home[i, here, :])
            home[i, here, :] = jnp.where(from_high[planes], high, own)

    def unpack_tile(t, planes=slice(0, 8)):
        for k in range(9):
            unpack(FIRST_ROW[t] + k, (2 * k, t), (2 * k + 1, t), planes)

    def collide_tile(step, t):
        source = home if step == 0 else flow

        def one_column(j, carry):
            cols = pl.ds(pl.multiple_of(j * 128, 128), 128)
            posts = collide([source[i, rows_of(t), cols] for i in range(19)], solid[rows_of(t), cols])
            for i in range(19):
                post[step, i, padded(t), cols] = posts[i]
            return carry

        lax.fori_loop(0, COLS, one_column, 0)

    started = {}

    def send(step, group, c, source, target):
        n = DIRS.index(c) + (18 if group == "inner" else 0)
        copy = pltpu.make_async_remote_copy(
            src_ref=source,
            dst_ref=target,
            send_sem=halo_send.at[step, n],
            recv_sem=halo_recv.at[step, n],
            device_id=beside(c),
            device_id_type=MESH,
        )
        copy.start()
        started.setdefault((step, group), []).append(copy)

    def await_halo(step, group):
        for copy in started[step, group]:
            copy.wait_recv()

    def send_x(step, sign):
        side = 0 if sign == 1 else 1
        exit_x = PAD + (BS - 1 if sign == 1 else 0)
        group = ("x", sign)
        for k, i in enumerate(with_component(0, sign)):
            out_x[step, side, k : k + 1, :] = post[step, i, exit_x : exit_x + 1, :]
        send(step, group, (sign, 0, 0), out_x.at[step, side], got_x.at[step, side])
        for k, i in enumerate(with_component(0, sign)):
            cx, cy, cz = VELS[i]
            if cy:
                cols = slice(LANES - 128, LANES) if cy == 1 else slice(0, 128)
                send(step, group, VELS[i], out_x.at[step, side, k : k + 1, cols], got_xy.at[step, i - 7])
            if cz:
                send(step, group, VELS[i], out_x.at[step, side, k : k + 1, :], got_xz.at[step, i - 11])

    def send_yz(step, group, tiles):
        at = 1 if group == "inner" else 0
        begin, end = SPOT[tiles[0]], SPOT[tiles[-1]] + 8
        for side, sign in enumerate((1, -1)):
            exit_z = ROW - 1 if sign == 1 else 0
            packed = None
            for n, t in enumerate(tiles):
                for k, i in enumerate(with_component(2, sign)):
                    q = 3 * (5 * n + k)
                    part = pltpu.roll(post[step, i, padded(t), :], (-sign * (ROW + q)) % LANES, 1)
                    for g in range(3):
                        piece = part[:, THIRD * g : THIRD * g + THIRD]
                        if g:
                            piece = pltpu.roll(piece, (-sign * g) % THIRD, 1)
                        if packed is None:
                            packed = piece
                        else:
                            packed = jnp.where(z_third == exit_z - sign * (q + g), piece, packed)
            out_z[step, at, side] = packed
            send(step, group, (0, 0, sign), out_z.at[step, at, side], got_z.at[step, at, side])
        for side, sign in enumerate((1, -1)):
            col = LANES - 128 if sign == 1 else 0
            for k, i in enumerate(with_component(1, sign)):
                for t in tiles:
                    out_y[step, at, side, k, SPOT[t] : SPOT[t] + 8, :] = post[
                        step, i, padded(t), col : col + 128
                    ]
            send(
                step,
                group,
                (0, sign, 0),
                out_y.at[step, at, side, :, begin:end, :],
                got_y.at[step, at, side, :, begin:end, :],
            )
        for i in range(15, 19):
            col = LANES - 128 if VELS[i][1] == 1 else 0
            for t in tiles:
                out_yz[step, at, i - 15, SPOT[t] : SPOT[t] + 8, :] = post[
                    step, i, padded(t), col : col + 128
                ]
            send(
                step,
                group,
                VELS[i],
                out_yz.at[step, at, i - 15, begin:end, :],
                got_yz.at[step, at, i - 15, begin:end, :],
            )

    def fill_yz(step, group, tiles):
        at = 1 if group == "inner" else 0
        tile_lane = lane[:, :128]
        for n, t in enumerate(tiles):
            spot = slice(SPOT[t], SPOT[t] + 8)
            for i in range(3, 19):
                cx, cy, cz = VELS[i]
                if cz:
                    exit_z = ROW - 1 if cz == 1 else 0
                    side = 0 if cz == 1 else 1
                    q = 3 * (5 * n + with_component(2, cz).index(i))
                    packed = got_z[step, at, side]
                    parts = [
                        pltpu.roll(packed, (cz * (q + g)) % THIRD, 1) if q + g else packed
                        for g in range(3)
                    ]
                    post[step, i, padded(t), :] = jnp.where(
                        z == exit_z, jnp.concatenate(parts, axis=1), post[step, i, padded(t), :]
                    )
                if cy:
                    side = 0 if cy == 1 else 1
                    col = LANES - 128 if cy == 1 else 0
                    cols = slice(col, col + 128)
                    leaves = tile_lane >= 128 - ROW if cy == 1 else tile_lane < ROW
                    if cz:
                        leaves = leaves & (z[:, cols] != exit_z)
                    k = with_component(1, cy).index(i)
                    post[step, i, padded(t), cols] = jnp.where(
                        leaves, got_y[step, at, side, k, spot, :], post[step, i, padded(t), cols]
                    )
                if cy and cz:
                    from_y = BS - 1 if cy == 1 else 0
                    slot = ((from_y - cz) % BS) * ROW + exit_z
                    source = from_y * ROW + exit_z
                    cols = slice(slot // 128 * 128, slot // 128 * 128 + 128)
                    edge = pltpu.roll(got_yz[step, at, i - 15, spot, :], (slot - source) % 128, 1)
                    post[step, i, padded(t), cols] = jnp.where(
                        tile_lane == slot % 128, edge, post[step, i, padded(t), cols]
                    )

    def fill_x(step, sign):
        side = 0 if sign == 1 else 1
        row_at = PAD - 1 if sign == 1 else PAD + BS
        one_lane = lane[0:1]
        for k, i in enumerate(with_component(0, sign)):
            cx, cy, cz = VELS[i]
            row = got_x[step, side, k : k + 1, :]
            if cz:
                exit_z = ROW - 1 if cz == 1 else 0
                edge = pltpu.roll(got_xz[step, i - 11], (-cz * ROW) % LANES, 1)
                row = jnp.where(z[0:1] == exit_z, edge, row)
            post[step, i, row_at : row_at + 1, :] = row
            if cy:
                col = LANES - 128 if cy == 1 else 0
                cols = slice(col, col + 128)
                leaves = one_lane[:, :128] >= 128 - ROW if cy == 1 else one_lane[:, :128] < ROW
                post[step, i, row_at : row_at + 1, cols] = jnp.where(
                    leaves, got_xy[step, i - 7], row[:, cols]
                )

    def stream(step, t, which=range(19)):
        target = fields if step == STEPS - 1 else flow
        for i in which:
            cx, cy, cz = VELS[i]
            v = post[step, i, padded(t, -cx), :]
            shift = (cy * ROW + cz) % LANES
            target[i, rows_of(t), :] = pltpu.roll(v, shift, 1) if shift else v

    loads[1].wait()
    pack(0, (18, 0), (18, 1))
    pack(1, (18, 2), None)
    loads[2].wait()
    pack_tile(0)
    pl.semaphore_wait(barrier, len(partners))
    send_ring(0, slice(0, FIRST_ROW[0] + 9), slice(0, 8))
    loads[3].wait()
    pack_tile(2)
    send_ring(1, slice(FIRST_ROW[2], FIRST_ROW[2] + 9), slice(0, 8))
    loads[4].wait()
    pack_tile(1)
    middle = slice(FIRST_ROW[1], FIRST_ROW[1] + 9)
    send_ring(2, middle, slice(0, 1))
    send_ring(3, middle, slice(7, 8))
    send_ring(4, middle, slice(1, 7))
    loads[5].wait()

    await_ring(0)
    unpack(0, (18, 0), (18, 1))
    unpack(1, (18, 2), None)
    unpack_tile(0)
    collide_tile(0, 0)
    send_x(0, -1)
    await_ring(1)
    unpack_tile(2)
    collide_tile(0, 2)
    send_x(0, 1)
    await_ring(2)
    await_ring(3)
    unpack_tile(1, slice(0, 1))
    unpack_tile(1, slice(7, 8))
    collide_tile(0, 1)
    send_yz(0, "outer", (0, 2, 1))
    await_halo(0, "outer")
    fill_yz(0, "outer", (0, 2, 1))
    await_halo(0, ("x", -1))
    fill_x(0, -1)
    stream(0, 2)
    collide_tile(1, 2)
    send_x(1, 1)
    stream(0, 0)

    await_ring(4)
    unpack_tile(1)
    collide_tile(0, 1)
    send_yz(0, "inner", (1,))

    await_halo(0, ("x", 1))
    fill_x(0, 1)
    for i in with_component(0, 1):
        cx, cy, cz = VELS[i]
        shift = (cy * ROW + cz) % LANES
        row = post[0, i, PAD - 1 : PAD, :]
        flow[i, 0:1, :] = pltpu.roll(row, shift, 1) if shift else row
    collide_tile(1, 0)
    send_x(1, -1)
    send_yz(1, "outer", (0, 2))

    await_halo(0, "inner")
    fill_yz(0, "inner", (1,))
    stream(0, 1)
    collide_tile(1, 1)
    send_yz(1, "inner", (1,))

    await_halo(1, "outer")
    fill_yz(1, "outer", (0, 2))
    await_halo(1, ("x", 1))
    fill_x(1, 1)
    stream(1, 0, [i for i in range(19) if VELS[i][0] != -1])
    await_halo(1, ("x", -1))
    fill_x(1, -1)
    stream(1, 2, [i for i in range(19) if VELS[i][0] != 1])
    await_halo(1, "inner")
    fill_yz(1, "inner", (1,))
    stream(1, 1)
    stream(1, 0, with_component(0, -1))
    stream(1, 2, with_component(0, 1))
    for copies in list(ring.values()) + list(started.values()):
        for copy in copies:
            copy.wait_send()


def per_device(popul, codes, solid):
    vmem = pl.BlockSpec(memory_space=pltpu.VMEM)
    fields = pl.pallas_call(
        kernel,
        out_shape=jax.ShapeDtypeStruct((19, BS, LANES), jnp.float32),
        in_specs=[pl.BlockSpec(memory_space=pltpu.HBM)] * 3,
        out_specs=vmem,
        scratch_shapes=[
            pltpu.SMEM((2,), jnp.int32),
            pltpu.VMEM((BS, LANES), jnp.int32),
            pltpu.VMEM((19, BS, LANES), jnp.float32),
            pltpu.VMEM((19, BS, LANES), jnp.float32),
            pltpu.VMEM((19, BS, LANES), jnp.float32),
            pltpu.VMEM((STEPS, 19, BS + 2 * PAD, LANES), jnp.float32),
        ]
        + [pltpu.VMEM((PACKED, 8, LANES), jnp.float32)] * 4
        + [
            pltpu.VMEM((STEPS, 2, 5, LANES), jnp.float32),
            pltpu.VMEM((STEPS, 2, 2, 5, BS, 128), jnp.float32),
            pltpu.VMEM((STEPS, 2, 2, 8, THIRD), jnp.float32),
            pltpu.VMEM((STEPS, 2, 4, BS, 128), jnp.float32),
        ]
        * 2
        + [
            pltpu.VMEM((STEPS, 4, 1, 128), jnp.float32),
            pltpu.VMEM((STEPS, 4, 1, LANES), jnp.float32),
            pltpu.SemaphoreType.DMA((6,)),
            pltpu.SemaphoreType.DMA((2, 5)),
            pltpu.SemaphoreType.DMA((2, 5)),
            pltpu.SemaphoreType.DMA((STEPS, 36)),
            pltpu.SemaphoreType.DMA((STEPS, 36)),
        ],
        compiler_params=pltpu.CompilerParams(
            collective_id=0, has_side_effects=True, vmem_limit_bytes=40 * 1024 * 1024
        ),
        cost_estimate=pl.CostEstimate(flops=14_000_000, bytes_accessed=4_500_000, transcendentals=0),
    )(codes, popul.reshape(19, BS, LANES), solid.reshape(BS, LANES))
    return fields.reshape(popul.shape)


def solution(mesh):
    placed = (
        P("gx", "gy", "gz", None, None),
        P(("gx", "gy", "gz")),
        P("gx", "gy", "gz", None, None),
    )
    return jax.shard_map(
        per_device,
        mesh=mesh,
        in_specs=placed,
        out_specs=P("gx", "gy", "gz", None, None),
        check_vma=False,
    )
```

time: 425 us -> 53.7 us (0.13); the launches traced: 420 us -> 53.5 us
  local copies, waits for them, and re-layouts: 156 us -> 4.47 us
  waiting for transfers between devices: 93.4 us -> 0 us
  matrix products: 93.1 us -> 0 us
  Pallas kernels: 0 us -> 49 us
  other arithmetic: 44.3 us -> 0 us
  starting transfers between devices: 32.5 us -> 0 us
    ppermute x16 -> x0, waiting for transfers between devices: 93.4 us -> none  [the longest x4 71.7 us: from_behind(): lax.ppermute(shard, axis, [(i, (i + by) % devices) for i in range(devices)])]
    dot_general x3 -> x0, matrix products: 93.1 us -> none  [select(): jnp.einsum('ks,cxysz->cxykz', table, blocks, precision=lax.Precision.HIGH...]
    slice x28 -> x0, local copies, waits for them, and re-layouts: 71.9 us -> none  [the longest x20 33.5 us: collide(): bounced = jnp.stack([f[o] for o in OPPOSITE])]
    pallas_call x0 -> x1, Pallas kernels: none -> 49 us  [per_device(): pl.pallas_call(kernel, out_shape=jax.ShapeDtypeStruct((19, BS, LANES), jn...]
    unnamed x56 -> x0, other arithmetic: 33.6 us -> none
    reshape x4 -> x0, local copies, waits for them, and re-layouts: 33.1 us -> none  [the longest x1 11.2 us: per_device(): lower_pop.reshape(19, edge, edge, count, edge)]
    ppermute x16 -> x0, starting transfers between devices: 32.5 us -> none  [the longest x6 18.2 us: extended(): after = lax.ppermute(initial, axis, down)]
    ppermute x4 -> x0, local copies, waits for them, and re-layouts: 23 us -> none  [the longest x2 11.5 us: extended(): after = lax.ppermute(initial, axis, down)]
  transfers between devices with their start and end apart: 16 -> 0, of which waited for: 7 -> 0; matrix products, arithmetic and copies ran while one was open for 32% -> 0% of each run, Pallas kernels for 0% -> 0%
where the time goes in v2:
time: 53.7 us; the launch traced here: 53.5 us
  Pallas kernels  49 us (91%)
  local copies, waits for them, and re-layouts  4.47 us (8%)
    pallas_call x1, Pallas kernels, per_device(): pl.pallas_call(kernel, out_shape=jax.ShapeDtypeStruct((19, BS, LANES), jn...  49 us
    unnamed x7, local copies, waits for them, and re-layouts  4.47 us

profile of v2, /device:TPU:1, one launch (start us, length us, event | category | flops | bytes accessed | tf_op | source)
XLA Modules:
  0.0 53.5 jit_solution(4998877828272841340)
XLA Ops:
  0.0 0.0 copy-start
  0.0 1.6 %copy-done = f32[1,1,1,456,1152]{4,3,2,1,0:T(8,128)S(1)} copy-done((f32[1,1,1,456,1152]{4,3,2,1,0:T(8,128)S(1)}, f32[1,1,1,456,1152]{4,3,2,1,0:T(8,128)}, u32[]{:S(2)}) %copy-start) | copy-done | bytes 2101272
  1.6 0.0 copy-start.1
  1.6 0.9 %copy-done.1 = s32[1,1,1,24,1152]{4,3,2,1,0:T(8,128)S(1)} copy-done((s32[1,1,1,24,1152]{4,3,2,1,0:T(8,128)S(1)}, s32[1,1,1,24,1152]{4,3,2,1,0:T(8,128)}, u32[]{:S(2)}) %copy-start.1) | copy-done | bytes 110616
  2.5 0.0 copy-start.2
  2.5 0.7 %copy-done.2 = s32[2]{0:T(128)S(1)} copy-done((s32[2]{0:T(128)S(1)}, s32[2]{0:T(128)}, u32[]{:S(2)}) %copy-start.2) | copy-done | bytes 32
  3.1 49.0 %shard_map.37 = f32[19,24,1152]{2,1,0:T(8,128)S(1)} custom-call(s32[2]{0:T(128)S(1)} %copy-done.2, f32[19,24,1152]{2,1,0:T(8,128)S(1)} %bitcast.4, s32[24,1152]{1,0:T(8,128)S(1)} %bitcast.5), custom_call_target="tpu_custom_call" | custom-call | flops 14000000 | bytes 4500000 | tf_op jit(solution)/shard_map/pallas_call | solution.py:449
  52.2 1.3 %copy.5 = f32[1,1,1,456,1152]{4,3,2,1,0:T(8,128)} copy(f32[1,1,1,456,1152]{4,3,2,1,0:T(8,128)S(1)} %bitcast.3) | data formatting | bytes 4202496
Async XLA Ops:
  0.0 1.6 %copy-start = (f32[1,1,1,456,1152]{4,3,2,1,0:T(8,128)S(1)}, f32[1,1,1,456,1152]{4,3,2,1,0:T(8,128)}, u32[]{:S(2)}) copy-start(f32[1,1,1,456,1152]{4,3,2,1,0:T(8,128)} %param.3) | copy-start | bytes 6303748
  1.6 0.9 %copy-start.1 = (s32[1,1,1,24,1152]{4,3,2,1,0:T(8,128)S(1)}, s32[1,1,1,24,1152]{4,3,2,1,0:T(8,128)}, u32[]{:S(2)}) copy-start(s32[1,1,1,24,1152]{4,3,2,1,0:T(8,128)} %param.5) | copy-start | bytes 331780
  2.5 0.7 %copy-start.2 = (s32[2]{0:T(128)S(1)}, s32[2]{0:T(128)}, u32[]{:S(2)}) copy-start(s32[2]{0:T(128)} %held_codes.1) | copy-start | bytes 28

commit v3 on v2

--- a/solution.py
+++ b/solution.py
@@ -209,7 +209,7 @@
                 post[step, i, padded(t), cols] = posts[i]
             return carry
 
-        lax.fori_loop(0, COLS, one_column, 0)
+        lax.fori_loop(0, COLS, one_column, 0, unroll=True)
 
     started = {}
 
@@ -254,11 +254,10 @@
             for n, t in enumerate(tiles):
                 for k, i in enumerate(with_component(2, sign)):
                     q = 3 * (5 * n + k)
-                    part = pltpu.roll(post[step, i, padded(t), :], (-sign * (ROW + q)) % LANES, 1)
+                    part = post[step, i, padded(t), :]
                     for g in range(3):
-                        piece = part[:, THIRD * g : THIRD * g + THIRD]
-                        if g:
-                            piece = pltpu.roll(piece, (-sign * g) % THIRD, 1)
+                        turned = pltpu.roll(part, (-sign * (ROW + q + g)) % LANES, 1)
+                        piece = turned[:, THIRD * g : THIRD * g + THIRD]
                         if packed is None:
                             packed = piece
                         else:
@@ -477,7 +476,7 @@
             pltpu.SemaphoreType.DMA((STEPS, 36)),
         ],
         compiler_params=pltpu.CompilerParams(
-            collective_id=0, has_side_effects=True, vmem_limit_bytes=40 * 1024 * 1024
+            collective_id=0, has_side_effects=True, vmem_limit_bytes=51 * 1024 * 1024
         ),
         cost_estimate=pl.CostEstimate(flops=14_000_000, bytes_accessed=4_500_000, transcendentals=0),
     )(codes, popul.reshape(19, BS, LANES), solid.reshape(BS, LANES))

time: 53.7 us -> 49.9 us (0.929)
  Pallas kernels: 49 us -> 46.9 us
  local copies, waits for them, and re-layouts: 4.47 us -> 2.87 us
    pallas_call x1, Pallas kernels: 49 us -> 46.9 us  [per_device(): pl.pallas_call(kernel, out_shape=jax.ShapeDtypeStruct((19, BS, LANES), jn...]
    unnamed x7 -> x5, local copies, waits for them, and re-layouts: 4.47 us -> 2.87 us
where the time goes in v3:
time: 49.9 us; the launch traced here: 49.7 us
  Pallas kernels  46.9 us (94%)
  local copies, waits for them, and re-layouts  2.87 us (6%)
    pallas_call x1, Pallas kernels, per_device(): pl.pallas_call(kernel, out_shape=jax.ShapeDtypeStruct((19, BS, LANES), jn...  46.9 us
    unnamed x5, local copies, waits for them, and re-layouts  2.87 us

profile of v3, /device:TPU:1, one launch (start us, length us, event | category | flops | bytes accessed | tf_op | source)
XLA Modules:
  0.0 49.7 jit_solution(5187020464625546343)
XLA Ops:
  0.0 0.0 copy-start
  0.0 0.9 %copy-done = s32[1,1,1,24,1152]{4,3,2,1,0:T(8,128)S(1)} copy-done((s32[1,1,1,24,1152]{4,3,2,1,0:T(8,128)S(1)}, s32[1,1,1,24,1152]{4,3,2,1,0:T(8,128)}, u32[]{:S(2)}) %copy-start) | copy-done | bytes 110616
  0.9 0.0 copy-start.1
  0.9 0.7 %copy-done.1 = s32[2]{0:T(128)S(1)} copy-done((s32[2]{0:T(128)S(1)}, s32[2]{0:T(128)}, u32[]{:S(2)}) %copy-start.1) | copy-done | bytes 32
  1.6 46.9 %shard_map.37 = f32[19,24,1152]{2,1,0:T(8,128)S(1)} custom-call(s32[2]{0:T(128)S(1)} %copy-done.1, f32[19,24,1152]{2,1,0:T(8,128)} %bitcast.5, s32[24,1152]{1,0:T(8,128)S(1)} %bitcast.4), custom_call_target="tpu_custom_call" | custom-call | flops 14000000 | bytes 4500000 | tf_op jit(solution)/shard_map/pallas_call | solution.py:448
  48.4 1.3 %copy.5 = f32[1,1,1,456,1152]{4,3,2,1,0:T(8,128)} copy(f32[1,1,1,456,1152]{4,3,2,1,0:T(8,128)S(1)} %bitcast.3) | data formatting | bytes 4202496
Async XLA Ops:
  0.0 0.9 %copy-start = (s32[1,1,1,24,1152]{4,3,2,1,0:T(8,128)S(1)}, s32[1,1,1,24,1152]{4,3,2,1,0:T(8,128)}, u32[]{:S(2)}) copy-start(s32[1,1,1,24,1152]{4,3,2,1,0:T(8,128)} %param.5) | copy-start | bytes 331780
  0.9 0.7 %copy-start.1 = (s32[2]{0:T(128)S(1)}, s32[2]{0:T(128)}, u32[]{:S(2)}) copy-start(s32[2]{0:T(128)} %held_codes.1) | copy-start | bytes 28

commit v4 on v3

--- a/solution.py
+++ b/solution.py
@@ -42,7 +42,10 @@
 THIRD = LANES // 3
 PAD = 8
 SPOT = {0: 0, 2: 8, 1: 16}
-FIRST_ROW = {0: 2, 2: 11, 1: 20}
+FIRST_ROW = {0: 1, 2: 10, 1: 19}
+FOLDED = 28
+HALF = LANES // 2
+HALF_COLS = 640
 PACKED = 29
 
 
@@ -152,9 +155,22 @@
 
     def pack(row, one, two):
         normal_one, swapped_one = both_orders(*one)
-        normal_two, swapped_two = (normal_one, swapped_one) if two is None else both_orders(*two)
+        normal_two, swapped_two = both_orders(*two)
         send_up[row] = jnp.where(first, swapped_one, normal_two)
         send_down[row] = jnp.where(first, normal_one, swapped_two)
+
+    def pack_folded(i, t):
+        normal, swapped = both_orders(i, t)
+        folded = pltpu.roll(normal, LANES - HALF, 1)
+        send_up[FOLDED] = jnp.where(first, swapped, folded)
+        send_down[FOLDED] = jnp.where(first, folded, swapped)
+
+    def unpack_folded(i, t):
+        low, high = got_up[FOLDED], got_down[FOLDED]
+        low = jnp.where(lane < HALF, low, pltpu.roll(low, HALF - BS, 1))
+        high = jnp.where(lane < HALF, high, pltpu.roll(high, HALF + BS, 1))
+        own = jnp.where(from_low, low, home[i, rows_of(t), :])
+        home[i, rows_of(t), :] = jnp.where(from_high, high, own)
 
     def pack_tile(t):
         for k in range(9):
@@ -162,14 +178,14 @@
 
     ring = {}
 
-    def send_ring(n, rows, planes):
+    def send_ring(n, rows, planes, cols=slice(0, LANES)):
         pair = []
         for way, (source, target, device) in enumerate(
             ((send_up, got_up, following), (send_down, got_down, previous))
         ):
             copy = pltpu.make_async_remote_copy(
-                src_ref=source.at[rows, planes, :],
-                dst_ref=target.at[rows, planes, :],
+                src_ref=source.at[rows, planes, cols],
+                dst_ref=target.at[rows, planes, cols],
                 send_sem=ring_send.at[way, n],
                 recv_sem=ring_recv.at[way, n],
                 device_id=device,
@@ -189,11 +205,10 @@
         here = slice(8 * t + planes.start, 8 * t + planes.stop)
         own = jnp.where(from_low[planes], low, home[i, here, :])
         home[i, here, :] = jnp.where(from_high[planes], pltpu.roll(high, BS, 1), own)
-        if two is not None:
-            i, t = two
-            here = slice(8 * t + planes.start, 8 * t + planes.stop)
-            own = jnp.where(from_low[planes], pltpu.roll(low, LANES - BS, 1), home[i, here, :])
-            home[i, here, :] = jnp.where(from_high[planes], high, own)
+        i, t = two
+        here = slice(8 * t + planes.start, 8 * t + planes.stop)
+        own = jnp.where(from_low[planes], pltpu.roll(low, LANES - BS, 1), home[i, here, :])
+        home[i, here, :] = jnp.where(from_high[planes], high, own)
 
     def unpack_tile(t, planes=slice(0, 8)):
         for k in range(9):
@@ -362,11 +377,12 @@
 
     loads[1].wait()
     pack(0, (18, 0), (18, 1))
-    pack(1, (18, 2), None)
+    pack_folded(18, 2)
     loads[2].wait()
     pack_tile(0)
     pl.semaphore_wait(barrier, len(partners))
     send_ring(0, slice(0, FIRST_ROW[0] + 9), slice(0, 8))
+    send_ring(5, slice(FOLDED, FOLDED + 1), slice(0, 8), slice(0, HALF_COLS))
     loads[3].wait()
     pack_tile(2)
     send_ring(1, slice(FIRST_ROW[2], FIRST_ROW[2] + 9), slice(0, 8))
@@ -379,8 +395,9 @@
     loads[5].wait()
 
     await_ring(0)
+    await_ring(5)
     unpack(0, (18, 0), (18, 1))
-    unpack(1, (18, 2), None)
+    unpack_folded(18, 2)
     unpack_tile(0)
     collide_tile(0, 0)
     send_x(0, -1)
@@ -394,6 +411,12 @@
     unpack_tile(1, slice(7, 8))
     collide_tile(0, 1)
     send_yz(0, "outer", (0, 2, 1))
+
+    await_ring(4)
+    unpack_tile(1)
+    collide_tile(0, 1)
+    send_yz(0, "inner", (1,))
+
     await_halo(0, "outer")
     fill_yz(0, "outer", (0, 2, 1))
     await_halo(0, ("x", -1))
@@ -401,20 +424,9 @@
     stream(0, 2)
     collide_tile(1, 2)
     send_x(1, 1)
-    stream(0, 0)
-
-    await_ring(4)
-    unpack_tile(1)
-    collide_tile(0, 1)
-    send_yz(0, "inner", (1,))
-
     await_halo(0, ("x", 1))
     fill_x(0, 1)
-    for i in with_component(0, 1):
-        cx, cy, cz = VELS[i]
-        shift = (cy * ROW + cz) % LANES
-        row = post[0, i, PAD - 1 : PAD, :]
-        flow[i, 0:1, :] = pltpu.roll(row, shift, 1) if shift else row
+    stream(0, 0)
     collide_tile(1, 0)
     send_x(1, -1)
     send_yz(1, "outer", (0, 2))
@@ -470,8 +482,8 @@
             pltpu.VMEM((STEPS, 4, 1, 128), jnp.float32),
             pltpu.VMEM((STEPS, 4, 1, LANES), jnp.float32),
             pltpu.SemaphoreType.DMA((6,)),
-            pltpu.SemaphoreType.DMA((2, 5)),
-            pltpu.SemaphoreType.DMA((2, 5)),
+            pltpu.SemaphoreType.DMA((2, 6)),
+            pltpu.SemaphoreType.DMA((2, 6)),
             pltpu.SemaphoreType.DMA((STEPS, 36)),
             pltpu.SemaphoreType.DMA((STEPS, 36)),
         ],

time: 49.9 us -> 48.4 us (0.970)
  Pallas kernels: 46.9 us -> 45.3 us
    pallas_call x1, Pallas kernels: 46.9 us -> 45.3 us  [per_device(): pl.pallas_call(kernel, out_shape=jax.ShapeDtypeStruct((19, BS, LANES), jn...]
where the time goes in v4:
time: 48.4 us; the launch traced here: 48.2 us
  Pallas kernels  45.3 us (94%)
  local copies, waits for them, and re-layouts  2.87 us (6%)
    pallas_call x1, Pallas kernels, per_device(): pl.pallas_call(kernel, out_shape=jax.ShapeDtypeStruct((19, BS, LANES), jn...  45.3 us
    unnamed x5, local copies, waits for them, and re-layouts  2.87 us

profile of v4, /device:TPU:1, one launch (start us, length us, event | category | flops | bytes accessed | tf_op | source)
XLA Modules:
  0.0 48.2 jit_solution(17342182729412230557)
XLA Ops:
  0.0 0.0 copy-start
  0.0 0.9 %copy-done = s32[1,1,1,24,1152]{4,3,2,1,0:T(8,128)S(1)} copy-done((s32[1,1,1,24,1152]{4,3,2,1,0:T(8,128)S(1)}, s32[1,1,1,24,1152]{4,3,2,1,0:T(8,128)}, u32[]{:S(2)}) %copy-start) | copy-done | bytes 110616
  0.9 0.0 copy-start.1
  0.9 0.7 %copy-done.1 = s32[2]{0:T(128)S(1)} copy-done((s32[2]{0:T(128)S(1)}, s32[2]{0:T(128)}, u32[]{:S(2)}) %copy-start.1) | copy-done | bytes 32
  1.6 45.3 %shard_map.37 = f32[19,24,1152]{2,1,0:T(8,128)S(1)} custom-call(s32[2]{0:T(128)S(1)} %copy-done.1, f32[19,24,1152]{2,1,0:T(8,128)} %bitcast.5, s32[24,1152]{1,0:T(8,128)S(1)} %bitcast.4), custom_call_target="tpu_custom_call" | custom-call | flops 14000000 | bytes 4500000 | tf_op jit(solution)/shard_map/pallas_call | solution.py:460
  46.9 1.3 %copy.5 = f32[1,1,1,456,1152]{4,3,2,1,0:T(8,128)} copy(f32[1,1,1,456,1152]{4,3,2,1,0:T(8,128)S(1)} %bitcast.3) | data formatting | bytes 4202496
Async XLA Ops:
  0.0 0.9 %copy-start = (s32[1,1,1,24,1152]{4,3,2,1,0:T(8,128)S(1)}, s32[1,1,1,24,1152]{4,3,2,1,0:T(8,128)}, u32[]{:S(2)}) copy-start(s32[1,1,1,24,1152]{4,3,2,1,0:T(8,128)} %param.5) | copy-start | bytes 331780
  0.9 0.7 %copy-start.1 = (s32[2]{0:T(128)S(1)}, s32[2]{0:T(128)}, u32[]{:S(2)}) copy-start(s32[2]{0:T(128)} %held_codes.1) | copy-start | bytes 28

commit v5 on v4

--- a/solution.py
+++ b/solution.py
@@ -251,18 +251,32 @@
         group = ("x", sign)
         for k, i in enumerate(with_component(0, sign)):
             out_x[step, side, k : k + 1, :] = post[step, i, exit_x : exit_x + 1, :]
+        for k, i in enumerate(with_component(0, sign)):
+            if VELS[i][2]:
+                send(step, group, VELS[i], out_x.at[step, side, k : k + 1, :], got_xz.at[step, i - 11])
         send(step, group, (sign, 0, 0), out_x.at[step, side], got_x.at[step, side])
         for k, i in enumerate(with_component(0, sign)):
-            cx, cy, cz = VELS[i]
+            cy = VELS[i][1]
             if cy:
                 cols = slice(LANES - 128, LANES) if cy == 1 else slice(0, 128)
                 send(step, group, VELS[i], out_x.at[step, side, k : k + 1, cols], got_xy.at[step, i - 7])
-            if cz:
-                send(step, group, VELS[i], out_x.at[step, side, k : k + 1, :], got_xz.at[step, i - 11])
 
     def send_yz(step, group, tiles):
         at = 1 if group == "inner" else 0
         begin, end = SPOT[tiles[0]], SPOT[tiles[-1]] + 8
+        for i in range(15, 19):
+            col = LANES - 128 if VELS[i][1] == 1 else 0
+            for t in tiles:
+                out_yz[step, at, i - 15, SPOT[t] : SPOT[t] + 8, :] = post[
+                    step, i, padded(t), col : col + 128
+                ]
+            send(
+                step,
+                group,
+                VELS[i],
+                out_yz.at[step, at, i - 15, begin:end, :],
+                got_yz.at[step, at, i - 15, begin:end, :],
+            )
         for side, sign in enumerate((1, -1)):
             exit_z = ROW - 1 if sign == 1 else 0
             packed = None
@@ -292,19 +306,6 @@
                 (0, sign, 0),
                 out_y.at[step, at, side, :, begin:end, :],
                 got_y.at[step, at, side, :, begin:end, :],
-            )
-        for i in range(15, 19):
-            col = LANES - 128 if VELS[i][1] == 1 else 0
-            for t in tiles:
-                out_yz[step, at, i - 15, SPOT[t] : SPOT[t] + 8, :] = post[
-                    step, i, padded(t), col : col + 128
-                ]
-            send(
-                step,
-                group,
-                VELS[i],
-                out_yz.at[step, at, i - 15, begin:end, :],
-                got_yz.at[step, at, i - 15, begin:end, :],
             )
 
     def fill_yz(step, group, tiles):

time: 48.4 us -> 48.1 us (level)
  Pallas kernels: 45.3 us -> 44.8 us
where the time goes in v5:
time: 48.1 us; the launch traced here: 47.7 us
  Pallas kernels  44.8 us (93%)
  local copies, waits for them, and re-layouts  2.87 us (6%)
    pallas_call x1, Pallas kernels, per_device(): pl.pallas_call(kernel, out_shape=jax.ShapeDtypeStruct((19, BS, LANES), jn...  44.8 us
    unnamed x5, local copies, waits for them, and re-layouts  2.87 us

profile of v5, /device:TPU:1, one launch (start us, length us, event | category | flops | bytes accessed | tf_op | source)
XLA Modules:
  0.0 47.7 jit_solution(14180635984927554561)
XLA Ops:
  0.0 0.0 copy-start
  0.0 0.9 %copy-done = s32[1,1,1,24,1152]{4,3,2,1,0:T(8,128)S(1)} copy-done((s32[1,1,1,24,1152]{4,3,2,1,0:T(8,128)S(1)}, s32[1,1,1,24,1152]{4,3,2,1,0:T(8,128)}, u32[]{:S(2)}) %copy-start) | copy-done | bytes 110616
  0.9 0.0 copy-start.1
  0.9 0.7 %copy-done.1 = s32[2]{0:T(128)S(1)} copy-done((s32[2]{0:T(128)S(1)}, s32[2]{0:T(128)}, u32[]{:S(2)}) %copy-start.1) | copy-done | bytes 32
  1.6 44.8 %shard_map.37 = f32[19,24,1152]{2,1,0:T(8,128)S(1)} custom-call(s32[2]{0:T(128)S(1)} %copy-done.1, f32[19,24,1152]{2,1,0:T(8,128)} %bitcast.5, s32[24,1152]{1,0:T(8,128)S(1)} %bitcast.4), custom_call_target="tpu_custom_call" | custom-call | flops 14000000 | bytes 4500000 | tf_op jit(solution)/shard_map/pallas_call | solution.py:461
  46.4 1.3 %copy.5 = f32[1,1,1,456,1152]{4,3,2,1,0:T(8,128)} copy(f32[1,1,1,456,1152]{4,3,2,1,0:T(8,128)S(1)} %bitcast.3) | data formatting | bytes 4202496
Async XLA Ops:
  0.0 0.9 %copy-start = (s32[1,1,1,24,1152]{4,3,2,1,0:T(8,128)S(1)}, s32[1,1,1,24,1152]{4,3,2,1,0:T(8,128)}, u32[]{:S(2)}) copy-start(s32[1,1,1,24,1152]{4,3,2,1,0:T(8,128)} %param.5) | copy-start | bytes 331780
  0.9 0.7 %copy-start.1 = (s32[2]{0:T(128)S(1)}, s32[2]{0:T(128)}, u32[]{:S(2)}) copy-start(s32[2]{0:T(128)} %held_codes.1) | copy-start | bytes 28
